TPU v7x, 256 devices: a whole 4x4x8 slice. The times are simulated.
256 devices in a mesh: tm: 16 (over x_hi, z), head: 16 (over y, x_lo, core).
Axes of the slice: x: 4 (x_hi: 2, x_lo: 2; x = x_hi * 2 + x_lo), y: 4, z: 8, core: 2. Of those that a mesh axis runs over, the one named last changes fastest.
Arguments:
- tokens: bfloat16 [64, 288, 1408], P('tm'), may hold values from -20 to 20
- norm_gain: float32 [1408], replicated, may hold values from 0.5 to 1.5
- norm_shift: float32 [1408], replicated, may hold values from -3 to 3
- w_qkv: bfloat16 [1408, 16, 264], P(None, 'head'), may hold values from -4 to 4
- output_weight: bfloat16 [1408, 1408], P('head'), may hold values from -0.625 to 0.625
Outputs:
- attended: bfloat16 [64, 288, 1408], P('tm', 'head')
All inputs are finite; a program needn't handle non-finite values.
Results may differ from a plain program's by a relative error of at most 0.024.
Values may be sent and summed in bfloat16 or wider, within the bound.
A program may use at most 64 MiB of HBM per device.

v0:
```python
import math

import jax
import jax.numpy as jnp
from jax import lax
from jax.sharding import PartitionSpec as P


def layer_norm(row_block, norm_gain, norm_shift):
    values = row_block.astype(jnp.float32)
    row_average = jnp.mean(values, axis=-1, keepdims=True)
    centred = values - row_average
    row_var = jnp.mean(centred * centred, axis=-1, keepdims=True)
    scaled = centred * lax.rsqrt(row_var + 1e-06) * norm_gain + norm_shift
    return scaled.astype(jnp.bfloat16)


def project(normed, w_qkv):
    width = normed.shape[-1]
    leading = normed.shape[:-1]
    flat_tokens = jnp.dot(
        normed.reshape(-1, width), w_qkv.reshape(width, -1), preferred_element_type=jnp.float32
    )
    return flat_tokens.astype(jnp.bfloat16).reshape(leading + w_qkv.shape[1:])


def attend(arrived_slab):
    head_size = arrived_slab.shape[-1] // 3
    query_block = arrived_slab[..., :head_size]
    key_rows = arrived_slab[..., head_size : 2 * head_size]
    value_rows = arrived_slab[..., 2 * head_size :]
    scores = jnp.einsum(
        "fphd,gphd->phfg", query_block, key_rows, preferred_element_type=jnp.float32
    )
    scores = scores * (1.0 / math.sqrt(head_size))
    row_max = jnp.max(scores, axis=-1, keepdims=True)
    exponent = jnp.exp(scores - row_max)
    probs = (exponent / jnp.sum(exponent, axis=-1, keepdims=True)).astype(jnp.bfloat16)
    result = jnp.einsum("phfg,gphd->pfhd", probs, value_rows, preferred_element_type=jnp.float32)
    return result.astype(jnp.bfloat16)


def on_device(tokens, norm_gain, norm_shift, w_qkv, output_weight):
    arrived = lax.all_to_all(tokens, "tm", split_axis=1, concat_axis=0, tiled=True)
    normed = layer_norm(arrived, norm_gain, norm_shift)
    packed = project(normed, w_qkv)
    head_outputs = attend(packed)
    local_rows = lax.all_to_all(head_outputs, "tm", split_axis=1, concat_axis=0, tiled=True)
    patch_count = local_rows.shape[0]
    frames_here = local_rows.shape[1]
    flat_tokens = local_rows.reshape(patch_count, frames_here, -1)
    summed = lax.psum_scatter(
        jnp.einsum(
            "qmz,ze->qme", flat_tokens, output_weight, preferred_element_type=jnp.float32
        ).astype(jnp.bfloat16),
        "head",
        scatter_dimension=0,
        tiled=True,
    ).astype(jnp.float32)
    return jnp.transpose(summed, (1, 0, 2)).astype(jnp.bfloat16)


def solution(mesh):
    return jax.shard_map(
        on_device,
        mesh=mesh,
        in_specs=(P("tm", None, None), P(), P(), P(None, "head", None), P("head", None)),
        out_specs=P("tm", "head", None),
        check_vma=False,
    )
```

profile of v0, /device:TPU:1, one launch (start us, length us, event | category | flops | bytes accessed | tf_op | source)
XLA Modules:
  0.0 280.4 jit_solution(10246658844020004343)
XLA Ops:
  6.5 3.7 %copy.22 = bf16[4,288,1408]{2,0,1:T(4,128)(2,1)S(1)} copy(bf16[4,288,1408]{2,1,0:T(8,128)(2,1)} %param.5) | data formatting | bytes 6488064 | tf_op args[0]
  10.2 86.4 %all_to_all.24 = bf16[4,288,1408]{2,0,1:T(4,128)(2,1)S(1)} all-to-all(bf16[4,288,1408]{2,0,1:T(4,128)(2,1)S(1)} %copy.22), channel_id=1, replica_groups=mesh['tm'=16,'head'=16] {'tm'}, dimensions={1} | all-to-all | bytes 6488064 | tf_op jit(solution)/shard_map/all_to_all | solution.py:44
  96.6 1.3 fusion.2
  97.9 2.3 fusion.5
  100.2 2.8 %fusion.8 = bf16[16,4,18,1408]{3,1,2,0:T(4,128)(2,1)S(1)} fusion(bf16[4,16,18,1408]{3,0,2,1:T(4,128)(2,1)S(1)} %bitcast.58, f32[1408]{0:T(1024)S(1)} %copy-done.2, f32[1408]{0:T(1024)S(1)} %copy-done.3, f32[16,4,18]{1,2,0:T(8,128)S(1)} %add_rsqrt_fusion, f32[16,4,18]{1,2,0:T(8,128)S(1)} %broadcast_multiply_fusion), kind=kLoop, calls=%fused_computation.9 | loop fusion | flops 9732096 | bytes 6508544 | tf_op jit(solution)/shard_map/convert_element_type | solution.py:15
  103.1 2.5 copy.23
  105.6 5.8 %convert_element_type.48 = bf16[1152,1408]{1,0:T(8,128)(2,1)} reshape(bf16[16,4,18,1408]{3,2,1,0:T(8,128)(2,1)} %copy.23) | data formatting | bytes 6488064 | tf_op jit(solution)/shard_map/convert_element_type | solution.py:15
  111.4 3.2 %convolution_convert_fusion.1 = bf16[1152,264]{0,1:T(8,128)(2,1)S(1)} fusion(bf16[1152,1408]{1,0:T(8,128)(2,1)} %convert_element_type.48, bf16[1408,1,264]{0,2,1:T(8,128)(2,1)S(1)} %copy-done), kind=kOutput, calls=%fused_computation.11 | convolution fusion | flops 856728576 | bytes 4595712 | tf_op jit(solution)/shard_map/dot_general | solution.py:21
  114.6 0.4 copy.24
  115.0 0.3 reshape.91
  115.3 0.3 fusion.18
  115.7 0.3 convolution_multiply_fusion
  116.0 0.3 fusion.19
  116.3 0.3 fusion.11
  116.6 0.2 copy.29
  116.8 17.0 %all_to_all.25 = bf16[18,64,1,88]{3,0,2,1:T(8,128)(2,1)S(1)} all-to-all(bf16[18,64,1,88]{3,0,2,1:T(8,128)(2,1)S(1)} %copy.29), channel_id=1, replica_groups=mesh['tm'=16,'head'=16] {'tm'}, dimensions={1} | all-to-all | bytes 405504 | tf_op jit(solution)/shard_map/all_to_all | solution.py:48
  133.8 0.1 copy.30
  134.0 1.0 convolution_convert_fusion
  135.0 3.4 %copy.32 = bf16[288,4,1408]{2,1,0:T(4,128)(2,1)} copy(bf16[288,4,1408]{2,0,1:T(8,128)(2,1)S(1)} %convolution_convert_fusion) | data formatting | bytes 6488064 | tf_op jit(solution)/shard_map/convert_element_type | solution.py:55
  138.3 0.0 all-reduce.3.cloned.1.call-update
  138.4 0.6 copy-done.4
  139.0 0.6 dynamic-slice
  140.2 131.6 %all-reduce.3.cloned.1.call-done = bf16[288,4,1408]{2,1,0:T(4,128)(2,1)} async-done(((bf16[288,4,1408]{2,1,0:T(4,128)(2,1)}), bf16[288,4,1408]{2,1,0:T(4,128)(2,1)}) %all-reduce.3.cloned.1.call-update) | async-done | bytes 3244048
  271.8 1.7 dynamic-slice_bitcast_fusion
  (12 shorter events, 0.1 us)
Async XLA Ops:
  6.5 104.9 %copy-start = (bf16[1408,1,264]{0,2,1:T(8,128)(2,1)S(1)}, bf16[1408,1,264]{0,2,1:T(8,128)(2,1)}, u32[]{:S(2)}) copy-start(bf16[1408,1,264]{0,2,1:T(8,128)(2,1)} %param.8) | copy-start | bytes 2230276
  6.5 265.3 %all-reduce.3.cloned.1.call-start = ((), (), s32[]{:S(2)}) async-start(), calls=%async_computation.2 | async-start | bytes 6488064
  96.6 3.7 %copy-start.2 = (f32[1408]{0:T(1024)S(1)}, f32[1408]{0:T(1024)}, u32[]{:S(2)}) copy-start(f32[1408]{0:T(1024)} %param.7) | copy-start | bytes 16900
  96.6 3.7 %copy-start.3 = (f32[1408]{0:T(1024)S(1)}, f32[1408]{0:T(1024)}, u32[]{:S(2)}) copy-start(f32[1408]{0:T(1024)} %param.6) | copy-start | bytes 16900
  115.9 18.0 %copy-start.1 = (bf16[88,1408]{1,0:T(8,128)(2,1)S(1)}, bf16[88,1408]{1,0:T(8,128)(2,1)}, u32[]{:S(2)}) copy-start(bf16[88,1408]{1,0:T(8,128)(2,1)} %param.9) | copy-start | bytes 743428
  138.3 0.7 copy-start.4
Sparse Core Ops, SparseCore 0:
  138.5 133.3 all-reduce.2
where the time goes:
time: 281 us; the launch traced here: 280 us
  waiting for transfers between devices  132 us (47%)
  blocking collectives  103 us (37%)
  local copies, waits for them, and re-layouts  19.7 us (7%)
  between operations  14.2 us (5%)
  other arithmetic  6.48 us (2%)
  matrix products  5.1 us (2%)
    unnamed x2, waiting for transfers between devices  132 us
    all_to_all x1, blocking collectives, on_device(): lax.all_to_all(tokens, 'tm', split_axis=1, concat_axis=0, tiled=True)  86.4 us
    all_to_all x1, blocking collectives, on_device(): lax.all_to_all(head_outputs, 'tm', split_axis=1, concat_axis=0, tiled=True)  17 us
    convert_element_type x2, local copies, waits for them, and re-layouts, layer_norm(): return scaled.astype(jnp.bfloat16)  8.31 us
  transfers between devices with their start and end apart: 1, of which 1 were waited for; matrix products, arithmetic and copies ran while one was open for 0% of the time, Pallas kernels for 0%

commit v1 on v0

v1 whole, which is shorter than its diff:
```python
import math

import jax
import jax.numpy as jnp
from jax import lax
from jax.sharding import PartitionSpec as P


def layer_norm(row_block, norm_gain, norm_shift):
    values = row_block.astype(jnp.float32)
    row_average = jnp.mean(values, axis=-1, keepdims=True)
    centred = values - row_average
    row_var = jnp.mean(centred * centred, axis=-1, keepdims=True)
    scaled = centred * lax.rsqrt(row_var + 1e-06) * norm_gain + norm_shift
    return scaled.astype(jnp.bfloat16)


def project(normed, w_qkv):
    width = normed.shape[-1]
    leading = normed.shape[:-1]
    flat_tokens = jnp.dot(
        normed.reshape(-1, width), w_qkv.reshape(width, -1), preferred_element_type=jnp.float32
    )
    return flat_tokens.astype(jnp.bfloat16).reshape(leading + (w_qkv.shape[2],))


def attend(arrived_slab):
    head_size = arrived_slab.shape[-1] // 3
    query_block = arrived_slab[..., :head_size]
    key_rows = arrived_slab[..., head_size : 2 * head_size]
    value_rows = arrived_slab[..., 2 * head_size :]
    scores = jnp.einsum(
        "fpd,gpd->pfg", query_block, key_rows, preferred_element_type=jnp.float32
    )
    scores = scores * (1.0 / math.sqrt(head_size))
    row_max = jnp.max(scores, axis=-1, keepdims=True)
    exponent = jnp.exp(scores - row_max)
    probs = (exponent / jnp.sum(exponent, axis=-1, keepdims=True)).astype(jnp.bfloat16)
    result = jnp.einsum("pfg,gpd->fpd", probs, value_rows, preferred_element_type=jnp.float32)
    return result.astype(jnp.bfloat16)


def on_device(tokens, norm_gain, norm_shift, w_qkv, output_weight):
    whole_weight = lax.all_gather(output_weight, "head", axis=0, tiled=True)
    packed = project(layer_norm(tokens, norm_gain, norm_shift), w_qkv)
    arrived = lax.all_to_all(packed, "tm", split_axis=1, concat_axis=0, tiled=True)
    head_outputs = attend(arrived)
    own_frames = lax.all_to_all(head_outputs, "tm", split_axis=0, concat_axis=1, tiled=True)
    own_rows = lax.all_to_all(own_frames, "head", split_axis=1, concat_axis=2, tiled=True)
    return jnp.einsum(
        "fpz,ze->fpe", own_rows, whole_weight, preferred_element_type=jnp.float32
    ).astype(jnp.bfloat16)


def solution(mesh):
    return jax.shard_map(
        on_device,
        mesh=mesh,
        in_specs=(P("tm", None, None), P(), P(), P(None, "head", None), P("head", None)),
        out_specs=P("tm", "head", None),
        check_vma=False,
    )
```

time: 281 us -> 96.6 us (0.34)
  waiting for transfers between devices: 132 us -> 0.73 us
  blocking collectives: 103 us -> 67.1 us
  local copies, waits for them, and re-layouts: 19.7 us -> 4.74 us
    unnamed x2 -> x1, waiting for transfers between devices: 132 us -> 0.71 us
    all_to_all x2 -> x3, blocking collectives: 103 us -> 67.1 us  [the longest x1 34.4 us: on_device(): lax.all_to_all(packed, 'tm', split_axis=1, concat_axis=0, tiled=True)]
    convert_element_type x5 -> x1, local copies, waits for them, and re-layouts: 13.8 us -> 0.76 us  [on_device(): return jnp.einsum('fpz,ze->fpe', own_rows, whole_weight, preferred_elemen...]
    unnamed x12 -> x8, local copies, waits for them, and re-layouts: 4.91 us -> 0.32 us
  transfers between devices with their start and end apart: 1 -> 1, of which waited for: 1 -> 0; matrix products, arithmetic and copies ran while one was open for 0% -> 11% of each run, Pallas kernels for 0% -> 0%
where the time goes in v1:
time: 96.6 us; the launch traced here: 96.4 us
  blocking collectives  67.1 us (69%)
  between operations  13.5 us (14%)
  matrix products  5.31 us (5%)
  other arithmetic  4.99 us (5%)
  local copies, waits for them, and re-layouts  4.74 us (5%)
    all_to_all x1, blocking collectives, on_device(): lax.all_to_all(packed, 'tm', split_axis=1, concat_axis=0, tiled=True)  34.4 us
    all_to_all x1, blocking collectives, on_device(): lax.all_to_all(head_outputs, 'tm', split_axis=0, concat_axis=1, tiled=True)  18.3 us
    all_to_all x1, blocking collectives, on_device(): lax.all_to_all(own_frames, 'head', split_axis=1, concat_axis=2, tiled=True)  14.4 us
    dot_general x1, matrix products, on_device(): jnp.einsum('fpz,ze->fpe', own_rows, whole_weight, preferred_element_type=...  2.89 us
    reduce_sum x1, other arithmetic, layer_norm(): row_average = jnp.mean(values, axis=-1, keepdims=True)  2.57 us
    reshape x2, local copies, waits for them, and re-layouts, project(): return flat_tokens.astype(jnp.bfloat16).reshape(leading + (w_qkv.shape[2],))  2.04 us
  transfers between devices with their start and end apart: 1, of which 0 were waited for; matrix products, arithmetic and copies ran while one was open for 11% of the time, Pallas kernels for 0%

profile of v1, /device:TPU:1, one launch (start us, length us, event | category | flops | bytes accessed | tf_op | source)
XLA Modules:
  0.0 96.4 jit_solution(1006693886358895018)
XLA Ops:
  6.5 0.0 copy-start
  6.5 0.0 all-gather.2.cloned.1.call-start
  6.5 0.7 all-gather.2.cloned.1.call-update
  7.3 2.6 %convert_reduce_fusion = f32[4,288]{1,0:T(4,128)S(1)} fusion(bf16[4,288,1408]{2,1,0:T(8,128)(2,1)} %param.5), kind=kLoop, calls=%fused_computation.2 | loop fusion | flops 3242880 | bytes 3248640 | tf_op jit(solution)/shard_map/reduce_sum | solution.py:11
  9.9 0.3 copy-done.1
  10.2 1.0 %fusion.3 = f32[4,288]{1,0:T(4,128)S(1)} fusion(bf16[4,288,1408]{2,1,0:T(8,128)(2,1)S(1)} %copy-done.1, f32[4,288]{1,0:T(4,128)S(1)} %broadcast_multiply_fusion), kind=kLoop, calls=%fused_computation.5 | loop fusion | flops 6486912 | bytes 3253248 | tf_op jit(solution)/shard_map/reduce_sum | solution.py:13
  11.2 1.4 %fusion.6 = bf16[4,288,1408]{2,1,0:T(8,128)(2,1)S(1)} fusion(bf16[4,288,1408]{2,1,0:T(8,128)(2,1)S(1)} %copy-done.1, f32[1408]{0:T(1024)S(1)} %copy-done.2, f32[1408]{0:T(1024)S(1)} %copy-done.3, f32[4,288]{1,0:T(4,128)S(1)} %add_rsqrt_fusion, f32[4,288]{1,0:T(4,128)S(1)} %broadcast_multiply_fusion), kind=kLoop, calls=%fused_computation.8 | loop fusion | flops 9732096 | bytes 6508544 | tf_op jit(solution)/shard_map/convert_element_type | solution.py:15
  12.6 1.3 %convolution_convert_fusion = bf16[1152,264]{0,1:T(8,128)(2,1)S(1)} fusion(bf16[1152,1408]{1,0:T(8,128)(2,1)S(1)} %bitcast.31, bf16[1408,1,264]{0,2,1:T(8,128)(2,1)S(1)} %copy-done), kind=kOutput, calls=%fused_computation.11 | convolution fusion | flops 856728576 | bytes 4595712 | tf_op jit(solution)/shard_map/dot_general | solution.py:21
  13.9 0.7 reshape.27
  14.6 1.3 %copy.16 = bf16[4,288,264]{2,0,1:T(4,128)(2,1)S(1)} copy(bf16[4,288,264]{1,0,2:T(4,128)(2,1)S(1)} %reshape.27) | data formatting | bytes 1216512 | tf_op jit(solution)/shard_map/reshape | solution.py:24
  15.9 34.4 %all_to_all.54 = bf16[4,288,264]{2,0,1:T(4,128)(2,1)S(1)} all-to-all(bf16[4,288,264]{2,0,1:T(4,128)(2,1)S(1)} %copy.16), channel_id=1, replica_groups=mesh['tm'=16,'head'=16] {'tm'}, dimensions={1} | all-to-all | bytes 1216512 | tf_op jit(solution)/shard_map/all_to_all | solution.py:46
  50.3 0.4 copy.17
  50.7 0.5 all_to_all.42
  51.2 0.4 fusion.26
  51.6 0.3 convolution_multiply_fusion
  52.0 0.4 fusion.14
  52.4 0.2 copy.19
  52.6 18.3 %all_to_all.55 = bf16[64,18,88]{2,1,0:T(8,128)(2,1)S(1)} all-to-all(bf16[64,18,88]{2,1,0:T(8,128)(2,1)S(1)} %copy.19), channel_id=1, replica_groups=mesh['tm'=16,'head'=16] {'tm'}, dimensions={0} | all-to-all | bytes 405504 | tf_op jit(solution)/shard_map/all_to_all | solution.py:48
  70.9 0.1 copy.20
  71.1 14.4 %all_to_all.56 = bf16[4,288,88]{2,0,1:T(4,128)(2,1)S(1)} all-to-all(bf16[4,288,88]{2,0,1:T(4,128)(2,1)S(1)} %bitcast.34), channel_id=1, replica_groups=mesh['tm'=16,'head'=16] {'head'}, dimensions={1} | all-to-all | bytes 405504 | tf_op jit(solution)/shard_map/all_to_all | solution.py:49
  85.5 0.4 reshape.29
  85.8 0.0 all-gather.2.cloned.1.call-done
  85.9 2.9 %fusion.9 = bf16[4,18,1408]{2,1,0:T(8,128)(2,1)S(1)} fusion(bf16[4,18,1408]{2,1,0:T(8,128)(2,1)S(1)} %reshape.29, bf16[1408,1408]{1,0:T(8,128)(2,1)} %all-gather.2.cloned.1.call-done), kind=kOutput, calls=%fused_computation.12 | convolution fusion | flops 285576192 | bytes 4370432 | tf_op jit(solution)/shard_map/fpz,ze->fpe/dot_general | solution.py:50
  88.8 0.8 copy.23
  (9 shorter events, 0.1 us)
Async XLA Ops:
  6.5 6.1 %copy-start = (bf16[1408,1,264]{0,2,1:T(8,128)(2,1)S(1)}, bf16[1408,1,264]{0,2,1:T(8,128)(2,1)}, u32[]{:S(2)}) copy-start(bf16[1408,1,264]{0,2,1:T(8,128)(2,1)} %param.8) | copy-start | bytes 2230276
  6.5 4.6 %copy-start.3 = (f32[1408]{0:T(1024)S(1)}, f32[1408]{0:T(1024)}, u32[]{:S(2)}) copy-start(f32[1408]{0:T(1024)} %param.6) | copy-start | bytes 16900
  6.5 4.6 %copy-start.2 = (f32[1408]{0:T(1024)S(1)}, f32[1408]{0:T(1024)}, u32[]{:S(2)}) copy-start(f32[1408]{0:T(1024)} %param.7) | copy-start | bytes 16900
  6.5 79.3 %all-gather.2.cloned.1.call-start = ((), (), s32[]{:S(2)}) async-start(), calls=%async_computation.3 | async-start | bytes 4212736 | tf_op jit(solution)/shard_map/all_gather | solution.py:44
  7.3 2.9 %copy-start.1 = (bf16[4,288,1408]{2,1,0:T(8,128)(2,1)S(1)}, bf16[4,288,1408]{2,1,0:T(8,128)(2,1)}, u32[]{:S(2)}) copy-start(bf16[4,288,1408]{2,1,0:T(8,128)(2,1)} %param.5) | copy-start | bytes 9732100
Sparse Core Ops, SparseCore 0:
  9.2 49.5 all-gather.1

commit v2 on v1

v2 whole, which is shorter than its diff:
```python
import math

import jax
import jax.numpy as jnp
from jax import lax
from jax.experimental import pallas as pl
from jax.experimental.pallas import tpu as pltpu
from jax.sharding import PartitionSpec as P

MESH = pl.DeviceIdType.MESH
D = 1408
HD = 88
FR = 4
PATCHES = 288
NT = 16
NH = 16
NZ = 8
HALF = PATCHES // 2
BLOCKS = 8
QA, QB = 5, 4
TA, TB = 2 * QA + 1, 2 * QB + 1
WROWS = 96
F32 = jnp.float32
BF16 = jnp.bfloat16


def kernel(
    tok_hbm, gain, shift, wq, wo, out,
    tok, wperm, packed, send_a, send_b, recv, ret_send, ret_recv, wbuf,
    tok_sem, p1_send, p1_recv, rt_send, rt_recv_a, rt_recv_b, loc_sem, w_send, w_recv,
):
    t = lax.axis_index("tm")
    h = lax.axis_index("head")
    xh, z = t // NZ, t % NZ
    chip, core = h // 2, h % 2
    y, xl = chip // 2, chip % 2
    is_a = xh == core

    tok_copies = [
        pltpu.make_async_copy(
            tok_hbm.at[:, pl.ds(k * HALF, HALF), :], tok.at[:, pl.ds(k * HALF, HALF), :], tok_sem.at[k]
        )
        for k in range(2)
    ]
    for copy in tok_copies:
        copy.start()

    def head_of(y_, xl_, core_):
        return ((y_ + 4) % 4) * 4 + xl_ * 2 + core_

    x_cross = ((1 - xh) * NZ + z, head_of(y, 1 - xl, core))
    barrier = pltpu.get_barrier_semaphore()

    @pl.loop(1, NT)
    def _(k):
        pl.semaphore_signal(barrier, inc=1, device_id=((t + k) % NT, h), device_id_type=MESH)
        pl.semaphore_signal(barrier, inc=1, device_id=(t, (h + k) % NH), device_id_type=MESH)

    pl.semaphore_signal(barrier, inc=1, device_id=x_cross, device_id_type=MESH)

    w = wq[...].astype(F32)
    wperm[:, 0:128] = jnp.concatenate([w[:, 0:88], w[:, 176:216]], axis=1).astype(BF16)
    wperm[:, 128:256] = jnp.concatenate([w[:, 88:176], w[:, 216:256]], axis=1).astype(BF16)
    wperm[:, 256:384] = jnp.concatenate(
        [w[:, 256:264], jnp.zeros((D, 120), F32)], axis=1
    ).astype(BF16)
    wbuf[h, pl.ds(0, WROWS), :] = jnp.concatenate(
        [wo[...].astype(F32), jnp.zeros((WROWS - HD, D), F32)], axis=0
    ).astype(BF16)

    @pl.loop(0, NH)
    def _(k):
        wbuf[k, pl.ds(WROWS, 128 - WROWS), :] = jnp.zeros((128 - WROWS, D), BF16)

    def project(k):
        tok_copies[k].wait()

        @pl.loop(0, FR)
        def _(f):
            values = tok[f, pl.ds(k * HALF, HALF), :].astype(F32)
            average = jnp.mean(values, axis=-1, keepdims=True)
            centred = values - average
            var = jnp.mean(centred * centred, axis=-1, keepdims=True)
            normed = centred * lax.rsqrt(var + 1e-06) * gain[...] + shift[...]
            packed[f] = jnp.dot(normed.astype(BF16), wperm[...], preferred_element_type=F32)

        parts = [packed[f].reshape(HALF // 8, 8, 384) for f in range(FR)]
        low = lax.broadcasted_iota(jnp.int32, parts[0].shape, 1) < 4
        turned = [pltpu.roll(part, 4, 1) for part in parts]
        even = jnp.concatenate(
            [jnp.where(low, parts[0], turned[1]), jnp.where(low, parts[2], turned[3])], axis=1
        )
        odd = jnp.concatenate(
            [jnp.where(low, turned[0], parts[1]), jnp.where(low, turned[2], parts[3])], axis=1
        )
        for b in range(BLOCKS // 2):
            for buf, first, count in ((send_a, 0, QA), (send_b, QA, QB)):
                rest = None
                for j in range(count):
                    q = 9 * b + first + j
                    tile = (odd if q % 2 else even)[q // 2]
                    at = k * (BLOCKS // 2) + b
                    buf[at, 1 + 2 * j] = tile[:, 0:128].astype(BF16)
                    buf[at, 2 + 2 * j] = tile[:, 128:256].astype(BF16)
                    left = tile[:, 256:384]
                    if j:
                        left = pltpu.roll(left, 8 * j, 1)
                    rest = left if rest is None else rest + left
                buf[at, 0] = rest.astype(BF16)

    def p1_copy(b, kind):
        buf, tiles = (send_a, TA) if kind == 0 else (send_b, TB)
        to_t = (core if kind == 0 else 1 - core) * NZ + (b + chip) % NZ
        src, dst = buf.at[b], recv.at[t, pl.ds(0, tiles)]
        remote = pltpu.make_async_remote_copy(
            src_ref=src, dst_ref=dst, send_sem=p1_send.at[2 * b + kind], recv_sem=p1_recv.at[t],
            device_id=(to_t, h), device_id_type=MESH,
        )
        return to_t == t, remote, pltpu.make_async_copy(src, dst, loc_sem.at[0])

    def p1_start(b, kind):
        own, remote, local = p1_copy(b, kind)

        @pl.when(own)
        def _():
            local.start()

        @pl.when(jnp.logical_not(own))
        def _():
            remote.start()

    def start_blocks(k):
        @pl.loop(0, BLOCKS // 2)
        def _(n):
            p1_start(k * (BLOCKS // 2) + n, 0)
            p1_start(k * (BLOCKS // 2) + n, 1)

    sib = (t, chip * 2 + 1 - core)
    x_near = (t, head_of(y, 1 - xl, core))
    y_up, y_down = (t, head_of(y + 1, xl, core)), (t, head_of(y - 1, xl, core))
    slot_x = head_of(y, 1 - xl, core)
    FULL, LOW, HIGH = (0, WROWS), (0, WROWS // 2), (WROWS // 2, WROWS // 2)

    def w_copy(slot, rows, to, n_send, n_recv):
        ref = wbuf.at[slot, pl.ds(rows[0], rows[1]), :]
        return pltpu.make_async_remote_copy(
            src_ref=ref, dst_ref=ref, send_sem=w_send.at[n_send], recv_sem=w_recv.at[n_recv],
            device_id=to, device_id_type=MESH,
        )

    def slot(dy, other_x, other_core):
        return head_of(y + dy, (1 - xl) if other_x else xl, (1 - core) if other_core else core)

    w_sends = []

    def w_start(copy):
        copy.start()
        w_sends.append(copy)

    def w_wait(slot_, rows, n_recv):
        w_copy(slot_, rows, sib, 0, n_recv).wait_recv()

    def w_first():
        w_start(w_copy(h, LOW, x_near, 0, 8))
        w_start(w_copy(h, HIGH, x_cross, 1, 9))
        w_start(w_copy(h, FULL, y_up, 2, 10))
        w_start(w_copy(h, FULL, y_down, 3, 11))
        w_start(w_copy(h, FULL, sib, 4, 0))

    def w_second():
        w_wait(slot_x, LOW, 8)
        w_wait(slot_x, HIGH, 9)
        w_start(w_copy(slot_x, FULL, y_up, 5, 12))
        w_start(w_copy(slot_x, FULL, y_down, 6, 13))
        w_start(w_copy(slot_x, FULL, sib, 7, 1))

    def w_third():
        for n, (dy, other_x, rows, to) in enumerate(
            ((-1, 0, LOW, y_up), (1, 0, HIGH, y_down), (-1, 1, LOW, y_up), (1, 1, HIGH, y_down))
        ):
            at = slot(dy, other_x, 0)
            w_wait(at, FULL, 10 + n)
            w_start(w_copy(at, rows, to, 8 + n, 14 + n))
            w_start(w_copy(at, FULL, sib, 12 + n, 2 + n))

    def w_fourth():
        for other_x in (0, 1):
            at = slot(2, other_x, 0)
            w_wait(at, LOW, 14 + 2 * other_x)
            w_wait(at, HIGH, 15 + 2 * other_x)
            w_start(w_copy(at, FULL, sib, 16 + other_x, 6 + other_x))

    def w_last():
        for n, (dy, other_x) in enumerate(
            ((0, 0), (0, 1), (-1, 0), (1, 0), (-1, 1), (1, 1), (2, 0), (2, 1))
        ):
            w_wait(slot(dy, other_x, 1), FULL, n)

    project(0)
    pl.semaphore_wait(barrier, 2 * (NT - 1) + 1)
    start_blocks(0)
    w_first()
    project(1)
    start_blocks(1)
    w_second()
    w_third()

    def p1_wait(tiles):
        @pl.loop(0, NT)
        def _(s):
            ref = recv.at[s, pl.ds(0, tiles)]

            @pl.when(s == t)
            def _():
                pltpu.make_async_copy(ref, ref, loc_sem.at[0]).wait()

            @pl.when(s != t)
            def _():
                pltpu.make_async_remote_copy(
                    src_ref=ref, dst_ref=ref, send_sem=p1_send.at[0], recv_sem=p1_recv.at[s],
                    device_id=(s, h), device_id_type=MESH,
                ).wait_recv()

    @pl.when(is_a)
    def _():
        p1_wait(TA)

    @pl.when(jnp.logical_not(is_a))
    def _():
        p1_wait(TB)

    rows = 16 * NT
    lane = lax.broadcasted_iota(jnp.int32, (rows, 128), 1)
    same = (
        lax.broadcasted_iota(jnp.int32, (rows, rows), 0) % 4
        == lax.broadcasted_iota(jnp.int32, (rows, rows), 1) % 4
    )

    def attend(j):
        first = recv[:, 1 + 2 * j].reshape(rows, 128)
        second = recv[:, 2 + 2 * j].reshape(rows, 128)
        rest = recv[:, 0].reshape(rows, 128)
        scores = lax.dot_general(
            first[:, :HD], second[:, :HD], (((1,), (1,)), ((), ())), preferred_element_type=F32
        ) * (1.0 / math.sqrt(HD))
        scores = jnp.where(same, scores, -jnp.inf)
        exponent = jnp.exp(scores - jnp.max(scores, axis=-1, keepdims=True))
        probs = (exponent / jnp.sum(exponent, axis=-1, keepdims=True)).astype(BF16)
        values = jnp.concatenate([first, second, rest], axis=1)
        mixed = jnp.dot(probs, values, preferred_element_type=F32)
        head = jnp.where(
            lane < 40,
            pltpu.roll(mixed[:, 0:128], 40, 1),
            jnp.where(
                lane < 80,
                pltpu.roll(mixed[:, 128:256], 80, 1),
                jnp.where(lane < HD, pltpu.roll(mixed[:, 256:384], 80 - 8 * j, 1), 0.0),
            ),
        )
        ret_send[:, j] = head.astype(BF16).reshape(NT, 16, 128)

    for j in range(QB):
        attend(j)

    @pl.when(is_a)
    def _():
        attend(QA - 1)

    to_chip = (z - chip + NZ) % NZ

    def ret_copy(to_t, to_core, src, dst, n_send, sem):
        to_h = to_chip * 2 + to_core
        own = jnp.logical_and(to_t == t, to_h == h)
        remote = pltpu.make_async_remote_copy(
            src_ref=src, dst_ref=dst, send_sem=rt_send.at[n_send], recv_sem=sem,
            device_id=(to_t, to_h), device_id_type=MESH,
        )
        return own, remote, pltpu.make_async_copy(src, dst, loc_sem.at[1])

    def ret_whole(to_t):
        return ret_copy(to_t, 0, ret_send.at[to_t], ret_recv.at[h], to_t, rt_recv_a.at[h])

    def ret_shared(to_t):
        return ret_copy(
            to_t, 1, ret_send.at[to_t, pl.ds(QB, 1)], ret_recv.at[h, pl.ds(0, 1)],
            NT + to_t, rt_recv_a.at[h],
        )

    def ret_rest(to_t):
        return ret_copy(
            to_t, 1, ret_send.at[to_t, pl.ds(0, QB)], ret_recv.at[h, pl.ds(1, QB)],
            to_t, rt_recv_b.at[h],
        )

    def start(triple):
        own, remote, local = triple

        @pl.when(own)
        def _():
            local.start()

        @pl.when(jnp.logical_not(own))
        def _():
            remote.start()

    def finish(triple):
        own, remote, _ = triple

        @pl.when(jnp.logical_not(own))
        def _():
            remote.wait_send()

    @pl.when(is_a)
    def _():
        @pl.loop(0, NT)
        def _(k):
            to_t = (t + k) % NT
            start(ret_whole(to_t))
            start(ret_shared(to_t))

    @pl.when(jnp.logical_not(is_a))
    def _():
        @pl.loop(0, NT)
        def _(k):
            start(ret_rest((t + k) % NT))

    w_fourth()
    w_last()

    def ret_wait(ref, from_t, from_h, sem):
        own = jnp.logical_and(from_t == t, from_h == h)

        @pl.when(own)
        def _():
            pltpu.make_async_copy(ref, ref, loc_sem.at[1]).wait()

        @pl.when(jnp.logical_not(own))
        def _():
            pltpu.make_async_remote_copy(
                src_ref=ref, dst_ref=ref, send_sem=rt_send.at[0], recv_sem=sem,
                device_id=(from_t, from_h), device_id_type=MESH,
            ).wait_recv()

    @pl.loop(0, NH)
    def _(g):
        from_z = (chip + g // 2) % NZ
        t_a = (g % 2) * NZ + from_z
        t_b = (1 - g % 2) * NZ + from_z

        @pl.when(core == 0)
        def _():
            ret_wait(ret_recv.at[g], t_a, g, rt_recv_a.at[g])

        @pl.when(core == 1)
        def _():
            ret_wait(ret_recv.at[g, pl.ds(0, 1)], t_a, g, rt_recv_a.at[g])
            ret_wait(ret_recv.at[g, pl.ds(1, QB)], t_b, g, rt_recv_b.at[g])

    left = jnp.concatenate([ret_recv[g].reshape(16 * QA, 128) for g in range(NH)], axis=1)
    total = jnp.dot(left, wbuf[...].reshape(NH * 128, D), preferred_element_type=F32)

    parts = total.reshape(2 * QA, 8, D)
    low = lax.broadcasted_iota(jnp.int32, (8, D), 0) < 4
    for f in range(FR):
        for pair in range(3):
            lo = parts[4 * pair + f // 2]
            hi = parts[4 * pair + 2 + f // 2] if pair < 2 else lo
            if f % 2 == 0:
                rows_ = jnp.where(low, lo, pltpu.roll(hi, 4, 0))
            else:
                rows_ = jnp.where(low, pltpu.roll(lo, 4, 0), hi)
            out[f, pl.ds(8 * pair, 8), :] = rows_

    @pl.loop(0, BLOCKS)
    def _(b):
        for kind in range(2):
            finish(p1_copy(b, kind))

    @pl.when(is_a)
    def _():
        @pl.loop(0, NT)
        def _(to_t):
            finish(ret_whole(to_t))
            finish(ret_shared(to_t))

    @pl.when(jnp.logical_not(is_a))
    def _():
        @pl.loop(0, NT)
        def _(to_t):
            finish(ret_rest(to_t))

    for copy in w_sends:
        copy.wait_send()


def on_device(tokens, norm_gain, norm_shift, w_qkv, output_weight):
    vmem = pl.BlockSpec(memory_space=pltpu.VMEM)
    dma = pltpu.SemaphoreType.DMA
    rows = pl.pallas_call(
        kernel,
        out_shape=jax.ShapeDtypeStruct((FR, 24, D), F32),
        in_specs=[pl.BlockSpec(memory_space=pl.ANY), vmem, vmem, vmem, vmem],
        out_specs=vmem,
        scratch_shapes=[
            pltpu.VMEM((FR, PATCHES, D), BF16),
            pltpu.VMEM((D, 384), BF16),
            pltpu.VMEM((FR, HALF, 384), F32),
            pltpu.VMEM((BLOCKS, TA, 16, 128), BF16),
            pltpu.VMEM((BLOCKS, TB, 16, 128), BF16),
            pltpu.VMEM((NT, TA, 16, 128), BF16),
            pltpu.VMEM((NT, QA, 16, 128), BF16),
            pltpu.VMEM((NH, QA, 16, 128), BF16),
            pltpu.VMEM((NH, 128, D), BF16),
            dma((2,)),
            dma((2 * BLOCKS,)),
            dma((NT,)),
            dma((2 * NT,)),
            dma((NH,)),
            dma((NH,)),
            dma((2,)),
            dma((18,)),
            dma((18,)),
        ],
        compiler_params=pltpu.CompilerParams(
            collective_id=0, has_side_effects=True, vmem_limit_bytes=48 * 1024 * 1024
        ),
        cost_estimate=pl.CostEstimate(
            flops=2 * FR * PATCHES * D * 264 + 2 * 72 * D * D,
            bytes_accessed=5_000_000,
            transcendentals=18 * 64 * 64,
        ),
    )(
        tokens,
        norm_gain.reshape(1, D),
        norm_shift.reshape(1, D),
        w_qkv.reshape(D, 3 * HD),
        output_weight,
    )
    core = lax.axis_index("head") % 2
    return lax.dynamic_slice_in_dim(rows, 2 * core, 18, axis=1).astype(BF16)


def solution(mesh):
    return jax.shard_map(
        on_device,
        mesh=mesh,
        in_specs=(P("tm", None, None), P(), P(), P(None, "head", None), P("head", None)),
        out_specs=P("tm", "head", None),
        check_vma=False,
    )
```

time: 96.6 us -> 52.5 us (0.54)
  the two profiles are of different devices: /device:TPU:1 before, /device:TPU:25 now
where the time goes in v2:
time: 52.5 us; the launch traced here: 52.3 us
  Pallas kernels  45.1 us (86%)
  local copies, waits for them, and re-layouts  7.19 us (14%)
    pallas_call x1, Pallas kernels, on_device(): pl.pallas_call(kernel, out_shape=jax.ShapeDtypeStruct((FR, 24, D), F32),...  45.1 us
    unnamed x5, local copies, waits for them, and re-layouts  4.97 us

profile of v2, /device:TPU:25, one launch (start us, length us, event | category | flops | bytes accessed | tf_op | source)
XLA Modules:
  0.0 52.3 jit_solution(13945722947207773046)
XLA Ops:
  0.0 0.7 %reshape.9.gain = f32[1,1408]{1,0:T(1,128)S(1)} reshape(f32[1408]{0:T(1024)} %param.6) | data formatting | bytes 11264 | tf_op jit(solution)/shard_map/reshape | solution.py:434
  0.7 0.7 %reshape.10.shift = f32[1,1408]{1,0:T(1,128)S(1)} reshape(f32[1408]{0:T(1024)} %param.7) | data formatting | bytes 11264 | tf_op jit(solution)/shard_map/reshape | solution.py:435
  1.4 2.1 %copy.8 = bf16[1408,1,264]{2,0,1:T(8,128)(2,1)S(1)} copy(bf16[1408,1,264]{0,2,1:T(8,128)(2,1)} %param.8) | data formatting | bytes 1486848 | tf_op args[3]
  3.5 0.0 copy-start
  3.5 1.9 %copy-done = bf16[4,288,1408]{2,1,0:T(8,128)(2,1)S(1)} copy-done((bf16[4,288,1408]{2,1,0:T(8,128)(2,1)S(1)}, bf16[4,288,1408]{2,1,0:T(8,128)(2,1)}, u32[]{:S(2)}) %copy-start) | copy-done | bytes 3244056
  5.4 0.0 copy-start.1
  5.4 0.9 %copy-done.1 = bf16[88,1408]{1,0:T(8,128)(2,1)S(1)} copy-done((bf16[88,1408]{1,0:T(8,128)(2,1)S(1)}, bf16[88,1408]{1,0:T(8,128)(2,1)}, u32[]{:S(2)}) %copy-start.1) | copy-done | bytes 247832
  6.4 45.1 %shard_map.55 = f32[4,24,1408]{2,1,0:T(8,128)S(1)} custom-call(bf16[4,288,1408]{2,1,0:T(8,128)(2,1)S(1)} %copy-done, f32[1,1408]{1,0:T(1,128)S(1)} %reshape.9.gain, f32[1,1408]{1,0:T(1,128)S(1)} %reshape.10.shift, bf16[1408,264]{1,0:T(8,128)(2,1)S(1)} %bitcast.1, bf16[88,1408]{1,0:T(8,128)(2,1)S(1)} %copy-done.1), custom_call_target="tpu_custom_call" | custom-call | flops 1141899264 | bytes 5000000 | tf_op jit(solution)/shard_map/pallas_call | solution.py:399
  51.5 0.1 dynamic-slice_convert_fusion
  51.5 0.8 %copy.9 = bf16[4,18,1408]{2,0,1:T(4,128)(2,1)} copy(bf16[4,18,1408]{2,1,0:T(8,128)(2,1)S(1)} %dynamic-slice_convert_fusion) | data formatting | bytes 405504 | tf_op jit(solution)/shard_map/convert_element_type | solution.py:440
Async XLA Ops:
  3.5 1.9 %copy-start = (bf16[4,288,1408]{2,1,0:T(8,128)(2,1)S(1)}, bf16[4,288,1408]{2,1,0:T(8,128)(2,1)}, u32[]{:S(2)}) copy-start(bf16[4,288,1408]{2,1,0:T(8,128)(2,1)} %tok_hbm.1) | copy-start | bytes 9732100
  5.4 0.9 %copy-start.1 = (bf16[88,1408]{1,0:T(8,128)(2,1)S(1)}, bf16[88,1408]{1,0:T(8,128)(2,1)}, u32[]{:S(2)}) copy-start(bf16[88,1408]{1,0:T(8,128)(2,1)} %wo.1) | copy-start | bytes 743428

commit v3 on v2

--- a/solution.py
+++ b/solution.py
@@ -25,9 +25,9 @@
 
 
 def kernel(
-    tok_hbm, gain, shift, wq, wo, out,
-    tok, wperm, packed, send_a, send_b, recv, ret_send, ret_recv, wbuf,
-    tok_sem, p1_send, p1_recv, rt_send, rt_recv_a, rt_recv_b, loc_sem, w_send, w_recv,
+    tok_hbm, gain_row, shift_row, wq_hbm, wo_hbm, out,
+    tok, wq, wo, wperm, packed, send_a, send_b, recv, ret_send, ret_recv, wbuf,
+    tok_sem, in_sem, p1_send, p1_recv, rt_send, rt_recv_a, rt_recv_b, loc_sem, w_send, w_recv,
 ):
     t = lax.axis_index("tm")
     h = lax.axis_index("head")
@@ -42,8 +42,12 @@
         )
         for k in range(2)
     ]
-    for copy in tok_copies:
-        copy.start()
+    wq_copy = pltpu.make_async_copy(wq_hbm, wq, in_sem.at[0])
+    wo_copy = pltpu.make_async_copy(wo_hbm, wo, in_sem.at[1])
+    tok_copies[0].start()
+    wq_copy.start()
+    tok_copies[1].start()
+    wo_copy.start()
 
     def head_of(y_, xl_, core_):
         return ((y_ + 4) % 4) * 4 + xl_ * 2 + core_
@@ -58,12 +62,12 @@
 
     pl.semaphore_signal(barrier, inc=1, device_id=x_cross, device_id_type=MESH)
 
+    wq_copy.wait()
     w = wq[...].astype(F32)
-    wperm[:, 0:128] = jnp.concatenate([w[:, 0:88], w[:, 176:216]], axis=1).astype(BF16)
-    wperm[:, 128:256] = jnp.concatenate([w[:, 88:176], w[:, 216:256]], axis=1).astype(BF16)
-    wperm[:, 256:384] = jnp.concatenate(
-        [w[:, 256:264], jnp.zeros((D, 120), F32)], axis=1
+    wperm[...] = jnp.concatenate(
+        [w[0:88], w[176:216], w[88:176], w[216:264], jnp.zeros((120, D), F32)], axis=0
     ).astype(BF16)
+    wo_copy.wait()
     wbuf[h, pl.ds(0, WROWS), :] = jnp.concatenate(
         [wo[...].astype(F32), jnp.zeros((WROWS - HD, D), F32)], axis=0
     ).astype(BF16)
@@ -71,6 +75,9 @@
     @pl.loop(0, NH)
     def _(k):
         wbuf[k, pl.ds(WROWS, 128 - WROWS), :] = jnp.zeros((128 - WROWS, D), BF16)
+
+    gain = gain_row[...].reshape(1, D)
+    shift = shift_row[...].reshape(1, D)
 
     def project(k):
         tok_copies[k].wait()
@@ -81,8 +88,10 @@
             average = jnp.mean(values, axis=-1, keepdims=True)
             centred = values - average
             var = jnp.mean(centred * centred, axis=-1, keepdims=True)
-            normed = centred * lax.rsqrt(var + 1e-06) * gain[...] + shift[...]
-            packed[f] = jnp.dot(normed.astype(BF16), wperm[...], preferred_element_type=F32)
+            normed = centred * lax.rsqrt(var + 1e-06) * gain + shift
+            packed[f] = lax.dot_general(
+                normed.astype(BF16), wperm[...], (((1,), (1,)), ((), ())), preferred_element_type=F32
+            )
 
         parts = [packed[f].reshape(HALF // 8, 8, 384) for f in range(FR)]
         low = lax.broadcasted_iota(jnp.int32, parts[0].shape, 1) < 4
@@ -395,15 +404,18 @@
 
 def on_device(tokens, norm_gain, norm_shift, w_qkv, output_weight):
     vmem = pl.BlockSpec(memory_space=pltpu.VMEM)
+    hbm = pl.BlockSpec(memory_space=pl.ANY)
     dma = pltpu.SemaphoreType.DMA
     rows = pl.pallas_call(
         kernel,
         out_shape=jax.ShapeDtypeStruct((FR, 24, D), F32),
-        in_specs=[pl.BlockSpec(memory_space=pl.ANY), vmem, vmem, vmem, vmem],
+        in_specs=[hbm, vmem, vmem, hbm, hbm],
         out_specs=vmem,
         scratch_shapes=[
             pltpu.VMEM((FR, PATCHES, D), BF16),
-            pltpu.VMEM((D, 384), BF16),
+            pltpu.VMEM((3 * HD, D), BF16),
+            pltpu.VMEM((HD, D), BF16),
+            pltpu.VMEM((384, D), BF16),
             pltpu.VMEM((FR, HALF, 384), F32),
             pltpu.VMEM((BLOCKS, TA, 16, 128), BF16),
             pltpu.VMEM((BLOCKS, TB, 16, 128), BF16),
@@ -411,6 +423,7 @@
             pltpu.VMEM((NT, QA, 16, 128), BF16),
             pltpu.VMEM((NH, QA, 16, 128), BF16),
             pltpu.VMEM((NH, 128, D), BF16),
+            dma((2,)),
             dma((2,)),
             dma((2 * BLOCKS,)),
             dma((NT,)),
@@ -422,7 +435,7 @@
             dma((18,)),
         ],
         compiler_params=pltpu.CompilerParams(
-            collective_id=0, has_side_effects=True, vmem_limit_bytes=48 * 1024 * 1024
+            collective_id=0, has_side_effects=True, vmem_limit_bytes=60 * 1024 * 1024
         ),
         cost_estimate=pl.CostEstimate(
             flops=2 * FR * PATCHES * D * 264 + 2 * 72 * D * D,
@@ -431,9 +444,9 @@
         ),
     )(
         tokens,
-        norm_gain.reshape(1, D),
-        norm_shift.reshape(1, D),
-        w_qkv.reshape(D, 3 * HD),
+        norm_gain,
+        norm_shift,
+        jnp.transpose(w_qkv, (1, 2, 0)).reshape(3 * HD, D),
         output_weight,
     )
     core = lax.axis_index("head") % 2

time: 52.5 us -> 48.3 us (0.920)
  the two profiles are of different devices: /device:TPU:25 before, /device:TPU:59 now
where the time goes in v3:
time: 48.3 us; the launch traced here: 48.2 us
  Pallas kernels  46.3 us (96%)
  local copies, waits for them, and re-layouts  1.86 us (4%)
    pallas_call x1, Pallas kernels, on_device(): pl.pallas_call(kernel, out_shape=jax.ShapeDtypeStruct((FR, 24, D), F32),...  46.3 us
    convert_element_type x2, local copies, waits for them, and re-layouts, on_device(): return lax.dynamic_slice_in_dim(rows, 2 * core, 18, axis=1).astype(BF16)  1.86 us

profile of v3, /device:TPU:59, one launch (start us, length us, event | category | flops | bytes accessed | tf_op | source)
XLA Modules:
  0.0 48.2 jit_solution(12620826750176137987)
XLA Ops:
  0.0 46.3 %shard_map.55 = f32[4,24,1408]{2,1,0:T(8,128)} custom-call(bf16[4,288,1408]{2,1,0:T(8,128)(2,1)} %tok_hbm.1, f32[1408]{0:T(1024)} %gain_row.1, f32[1408]{0:T(1024)} %shift_row.1, bf16[264,1408]{1,0:T(8,128)(2,1)} %bitcast.3, bf16[88,1408]{1,0:T(8,128)(2,1)} %wo_hbm.1), custom_call_target="tpu_custom_call" | custom-call | flops 1141899264 | bytes 5000000 | tf_op jit(solution)/shard_map/pallas_call | solution.py:409
  46.3 1.1 %dynamic-slice_convert_fusion = bf16[4,18,1408]{2,1,0:T(8,128)(2,1)S(1)} fusion(f32[4,24,1408]{2,1,0:T(8,128)} %shard_map.55, s32[]{:T(128)S(6)} %select_n.11), kind=kLoop, calls=%fused_computation | loop fusion | bytes 405508 | tf_op jit(solution)/shard_map/convert_element_type | solution.py:453
  47.4 0.8 %copy.7 = bf16[4,18,1408]{2,0,1:T(4,128)(2,1)} copy(bf16[4,18,1408]{2,1,0:T(8,128)(2,1)S(1)} %dynamic-slice_convert_fusion) | data formatting | bytes 405504 | tf_op jit(solution)/shard_map/convert_element_type | solution.py:453

commit v4 on v3

v4 whole, which is shorter than its diff:
```python
import math

import jax
import jax.numpy as jnp
from jax import lax
from jax.experimental import pallas as pl
from jax.experimental.pallas import tpu as pltpu
from jax.sharding import PartitionSpec as P

MESH = pl.DeviceIdType.MESH
D = 1408
HD = 88
FR = 4
PATCHES = 288
NT = 16
NH = 16
NZ = 8
HALF = PATCHES // 2
BLOCKS = 8
QA, QB = 5, 4
TA, TB = 2 * QA + 1, 2 * QB + 1
QFIRST = 3
TFIRST = 2 * QFIRST + 1
RT = 4
WROWS = 96
F32 = jnp.float32
BF16 = jnp.bfloat16


def kernel(
    tok_hbm, gain_row, shift_row, wq_hbm, wo_hbm, out,
    tok, wq, wo, wperm, packed, send, recv, ret_send, ret_recv, wbuf, rows_out,
    tok_sem, in_sem, p1_send, p1_recv, rt_send, rt_recv, w_send, w_recv,
):
    t = lax.axis_index("tm")
    h = lax.axis_index("head")
    xh, z = t // NZ, t % NZ
    chip, core = h // 2, h % 2
    y, xl = chip // 2, chip % 2
    is_a = xh == core

    halves = ((z + xl) % 2, (z + xl + 1) % 2)

    def z_of(block, y_, xl_):
        return ((block % 4 - y_ + 4) % 4) * 2 + (block // 4 + xl_) % 2

    def half_rows(n):
        return pl.ds(pl.multiple_of(halves[n] * HALF, 16), HALF)

    tok_copies = [
        pltpu.make_async_copy(
            tok_hbm.at[:, half_rows(n), :], tok.at[:, half_rows(n), :], tok_sem.at[n]
        )
        for n in range(2)
    ]
    wq_copy = pltpu.make_async_copy(wq_hbm, wq, in_sem.at[0])
    wo_copy = pltpu.make_async_copy(wo_hbm, wo, in_sem.at[1])
    tok_copies[0].start()
    wq_copy.start()
    tok_copies[1].start()
    wo_copy.start()

    def head_of(y_, xl_, core_):
        return ((y_ + 4) % 4) * 4 + xl_ * 2 + core_

    x_cross = ((1 - xh) * NZ + z, head_of(y, 1 - xl, core))
    barrier = pltpu.get_barrier_semaphore()

    @pl.loop(1, NT)
    def _(k):
        pl.semaphore_signal(barrier, inc=1, device_id=((t + k) % NT, h), device_id_type=MESH)
        pl.semaphore_signal(barrier, inc=1, device_id=(t, (h + k) % NH), device_id_type=MESH)

    pl.semaphore_signal(barrier, inc=1, device_id=x_cross, device_id_type=MESH)

    wq_copy.wait()
    w = wq[...].astype(F32)
    wperm[...] = jnp.concatenate(
        [w[0:88], w[176:216], w[88:176], w[216:264], jnp.zeros((120, D), F32)], axis=0
    ).astype(BF16)
    gain = gain_row[...].reshape(1, D)
    shift = shift_row[...].reshape(1, D)

    def project(n):
        tok_copies[n].wait()

        @pl.loop(0, FR)
        def _(f):
            values = tok[f, half_rows(n), :].astype(F32)
            average = jnp.mean(values, axis=-1, keepdims=True)
            centred = values - average
            var = jnp.mean(centred * centred, axis=-1, keepdims=True)
            normed = centred * lax.rsqrt(var + 1e-06) * gain + shift
            tok[f, half_rows(n), :] = normed.astype(BF16)

        packed[...] = lax.dot_general(
            tok[:, half_rows(n), :].reshape(FR * HALF, D), wperm[...],
            (((1,), (1,)), ((), ())), preferred_element_type=F32,
        ).reshape(FR, HALF, 384)

        parts = [packed[f].reshape(HALF // 8, 8, 384) for f in range(FR)]
        low = lax.broadcasted_iota(jnp.int32, parts[0].shape, 1) < 4
        turned = [pltpu.roll(part, 4, 1) for part in parts]
        even = jnp.concatenate(
            [jnp.where(low, parts[0], turned[1]), jnp.where(low, parts[2], turned[3])], axis=1
        )
        odd = jnp.concatenate(
            [jnp.where(low, turned[0], parts[1]), jnp.where(low, turned[2], parts[3])], axis=1
        )
        for b in range(BLOCKS // 2):
            for kind, first, count in ((0, 0, QA), (1, QA, QB)):
                rest = None
                for j in range(count):
                    q = 9 * b + first + j
                    tile = (odd if q % 2 else even)[q // 2]
                    at = halves[n] * (BLOCKS // 2) + b
                    send[at, kind, 1 + 2 * j] = tile[:, 0:128].astype(BF16)
                    send[at, kind, 2 + 2 * j] = tile[:, 128:256].astype(BF16)
                    left = tile[:, 256:384]
                    if j:
                        left = pltpu.roll(left, 8 * j, 1)
                    rest = left if rest is None else rest + left
                send[at, kind, 0] = rest.astype(BF16)

    def p1_to(b, kind):
        return jnp.where(kind == 0, core, 1 - core) * NZ + z_of(b, y, xl)

    def p1_copy(b, kind, group, tiles):
        src, dst = send.at[b, kind, tiles], recv.at[t, tiles]
        to_t = p1_to(b, kind)
        remote = pltpu.make_async_remote_copy(
            src_ref=src, dst_ref=dst, send_sem=p1_send.at[group, 2 * b + kind],
            recv_sem=p1_recv.at[group], device_id=(to_t, h), device_id_type=MESH,
        )
        return to_t == t, remote, lambda: pltpu.make_async_copy(src, dst, p1_recv.at[group])

    def start(triple):
        own, remote, local = triple

        @pl.when(own)
        def _():
            local().start()

        @pl.when(jnp.logical_not(own))
        def _():
            remote.start()

    def finish(triple):
        own, remote, _ = triple

        @pl.when(jnp.logical_not(own))
        def _():
            remote.wait_send()

    def p1_first(b, kind):
        return p1_copy(b, kind, 0, FIRST)

    def p1_second(b, kind):
        return p1_copy(b, kind, 1, SECOND[kind])

    FIRST = pl.ds(0, TFIRST)
    SECOND = (pl.ds(TFIRST, TA - TFIRST), pl.ds(TFIRST, TB - TFIRST))

    def block_at(n, step):
        off = step + 2 if n == 0 else step + 1 + z % 2
        return halves[n] * (BLOCKS // 2) + (z // 2 + off + y) % (BLOCKS // 2)

    def start_first(n):
        @pl.loop(0, BLOCKS // 2)
        def _(step):
            b = block_at(n, step)
            start(p1_first(b, jnp.where(is_a, 1, 0)))
            start(p1_first(b, jnp.where(is_a, 0, 1)))

    def start_second(n):
        @pl.loop(0, BLOCKS // 2)
        def _(step):
            b = block_at(n, step)
            start(p1_second(b, 0))
            start(p1_second(b, 1))

    sib = (t, chip * 2 + 1 - core)
    x_near = (t, head_of(y, 1 - xl, core))
    y_up, y_down = (t, head_of(y + 1, xl, core)), (t, head_of(y - 1, xl, core))
    slot_x = head_of(y, 1 - xl, core)
    FULL, LOW, HIGH = (0, WROWS), (0, WROWS // 2), (WROWS // 2, WROWS // 2)

    def w_copy(slot, rows, to, n_send, n_recv):
        ref = wbuf.at[slot, pl.ds(rows[0], rows[1]), :]
        return pltpu.make_async_remote_copy(
            src_ref=ref, dst_ref=ref, send_sem=w_send.at[n_send], recv_sem=w_recv.at[n_recv],
            device_id=to, device_id_type=MESH,
        )

    def slot(dy, other_x, other_core):
        return head_of(y + dy, (1 - xl) if other_x else xl, (1 - core) if other_core else core)

    w_sends = []

    def w_start(copy):
        copy.start()
        w_sends.append(copy)

    def w_wait(slot_, rows, n_recv):
        w_copy(slot_, rows, sib, 0, n_recv).wait_recv()

    def w_first():
        w_start(w_copy(h, LOW, x_near, 0, 8))
        w_start(w_copy(h, HIGH, x_cross, 1, 9))
        w_start(w_copy(h, FULL, y_up, 2, 10))
        w_start(w_copy(h, FULL, y_down, 3, 11))
        w_start(w_copy(h, FULL, sib, 4, 0))

    def w_second():
        w_wait(slot_x, LOW, 8)
        w_wait(slot_x, HIGH, 9)
        w_start(w_copy(slot_x, FULL, y_up, 5, 12))
        w_start(w_copy(slot_x, FULL, y_down, 6, 13))
        w_start(w_copy(slot_x, FULL, sib, 7, 1))

    def w_relay(other_x):
        for n, (dy, rows, to) in enumerate(((-1, LOW, y_up), (1, HIGH, y_down))):
            n += 2 * other_x
            at = slot(dy, other_x, 0)
            w_wait(at, FULL, 10 + n)
            w_start(w_copy(at, rows, to, 8 + n, 14 + n))
            w_start(w_copy(at, FULL, sib, 12 + n, 2 + n))

    def w_fourth():
        for other_x in (0, 1):
            at = slot(2, other_x, 0)
            w_wait(at, LOW, 14 + 2 * other_x)
            w_wait(at, HIGH, 15 + 2 * other_x)
            w_start(w_copy(at, FULL, sib, 16 + other_x, 6 + other_x))

    def w_last():
        for n, (dy, other_x) in enumerate(
            ((0, 0), (0, 1), (-1, 0), (1, 0), (-1, 1), (1, 1), (2, 0), (2, 1))
        ):
            w_wait(slot(dy, other_x, 1), FULL, n)

    project(0)
    pl.semaphore_wait(barrier, 2 * (NT - 1) + 1)
    start_first(0)
    wo_copy.wait()
    wbuf[h, pl.ds(0, WROWS), :] = jnp.concatenate(
        [wo[...].astype(F32), jnp.zeros((WROWS - HD, D), F32)], axis=0
    ).astype(BF16)

    @pl.loop(0, NH)
    def _(k):
        wbuf[k, pl.ds(WROWS, 128 - WROWS), :] = jnp.zeros((128 - WROWS, D), BF16)

    w_first()
    project(1)
    start_first(1)
    start_second(0)
    start_second(1)
    w_second()
    w_relay(0)

    def p1_wait(group, tiles):
        ref = recv.at[:, tiles]
        pltpu.make_async_copy(ref, ref, p1_recv.at[group]).wait()

    rows = 16 * NT
    lane = lax.broadcasted_iota(jnp.int32, (rows, 128), 1)
    same = (
        lax.broadcasted_iota(jnp.int32, (rows, rows), 0) % 4
        == lax.broadcasted_iota(jnp.int32, (rows, rows), 1) % 4
    )

    def attend(j):
        first = recv[:, 1 + 2 * j].reshape(rows, 128)
        second = recv[:, 2 + 2 * j].reshape(rows, 128)
        rest = recv[:, 0].reshape(rows, 128)
        scores = lax.dot_general(
            first[:, :HD], second[:, :HD], (((1,), (1,)), ((), ())), preferred_element_type=F32
        ) * (1.0 / math.sqrt(HD))
        scores = jnp.where(same, scores, -jnp.inf)
        exponent = jnp.exp(scores - jnp.max(scores, axis=-1, keepdims=True))
        probs = (exponent / jnp.sum(exponent, axis=-1, keepdims=True)).astype(BF16)
        values = jnp.concatenate([first, second, rest], axis=1)
        mixed = jnp.dot(probs, values, preferred_element_type=F32)
        return mixed

    def in_order(first, second, rest, turn):
        return jnp.where(
            lane < 40,
            pltpu.roll(first, 40, 1),
            jnp.where(lane < 80, pltpu.roll(second, 80, 1), pltpu.roll(rest, turn, 1)),
        )

    def straight(mixed, j):
        return in_order(
            mixed[:, 0:128], mixed[:, 128:256], mixed[:, 256:384], (80 - 8 * j) % 128
        )

    def put(n, tile):
        ret_send[:, n] = tile.astype(BF16).reshape(NT, 16, 128)

    to_chip = ((z + xl) % 2) * 4 + (z // 2 + y) % 4

    def ret_copy(to_t, to_core, first, count, sem):
        tiles = pl.ds(first, count)
        to_h = to_chip * 2 + to_core
        own = jnp.logical_and(to_t == t, to_h == h)
        src, dst = ret_send.at[to_t, tiles], ret_recv.at[h, tiles]
        remote = pltpu.make_async_remote_copy(
            src_ref=src, dst_ref=dst, send_sem=rt_send.at[sem, to_t], recv_sem=rt_recv.at[0],
            device_id=(to_t, to_h), device_id_type=MESH,
        )
        return own, remote, lambda: pltpu.make_async_copy(src, dst, rt_recv.at[0])

    def far_first(k):
        n, away = k // 2, (k // 2 + 1) // 2
        off = jnp.where(n % 2 == 0, NZ // 2 - away, NZ // 2 + away)
        return ((xh + 1 - k % 2) % 2) * NZ + (z + off) % NZ

    def ret_first(to_t):
        return ret_copy(to_t, jnp.where(is_a, 0, 1), 0, 2, 0)

    def ret_second_a(to_t):
        return ret_copy(to_t, 0, 2, 2, 1)

    def ret_second_b(to_t):
        return ret_copy(to_t, 1, 2, 1, 1)

    def ret_shared(to_t):
        return ret_copy(to_t, 1, 3, 1, 2)

    p1_wait(0, FIRST)

    mixed2 = attend(2)
    put(0, jnp.where(lane < HD, straight(attend(0), 0), mixed2[:, 0:128]))
    put(1, jnp.where(lane < HD, straight(attend(1), 1), mixed2[:, 128:256]))
    rest2 = pltpu.roll(mixed2[:, 256:384], 72, 1)

    @pl.loop(0, NT)
    def _(k):
        start(ret_first(far_first(k)))

    w_relay(1)

    @pl.when(is_a)
    def _():
        p1_wait(1, SECOND[0])
        put(3, straight(attend(4), 4))

    @pl.when(jnp.logical_not(is_a))
    def _():
        p1_wait(1, SECOND[1])

    put(2, jnp.where(lane < HD, straight(attend(3), 3), rest2))

    @pl.when(is_a)
    def _():
        @pl.loop(0, NT)
        def _(k):
            to_t = far_first(k)
            start(ret_second_a(to_t))
            start(ret_shared(to_t))

    @pl.when(jnp.logical_not(is_a))
    def _():
        @pl.loop(0, NT)
        def _(k):
            start(ret_second_b(far_first(k)))

    w_fourth()
    w_last()

    @pl.loop(0, BLOCKS)
    def _(b):
        for kind in range(2):
            finish(p1_first(b, kind))
            finish(p1_second(b, kind))

    @pl.loop(0, NT)
    def _(to_t):
        finish(ret_first(to_t))

    @pl.when(is_a)
    def _():
        @pl.loop(0, NT)
        def _(to_t):
            finish(ret_second_a(to_t))
            finish(ret_shared(to_t))

    @pl.when(jnp.logical_not(is_a))
    def _():
        @pl.loop(0, NT)
        def _(to_t):
            finish(ret_second_b(to_t))

    for copy in w_sends:
        copy.wait_send()

    pltpu.make_async_copy(ret_recv, ret_recv, rt_recv.at[0]).wait()

    tiles = [ret_recv[:, n] for n in range(RT)]
    parts = [tile.reshape(rows, 128).astype(F32) for tile in tiles[:3]]
    third = in_order(parts[0], parts[1], parts[2], 120).astype(BF16).reshape(NH, 16, 128)
    left = jnp.concatenate(
        [
            jnp.concatenate([quad[g] for g in range(NH)], axis=1)
            for quad in (tiles[0], tiles[1], third, tiles[2], tiles[3])
        ],
        axis=0,
    )
    total = jnp.dot(left, wbuf[...].reshape(NH * 128, D), preferred_element_type=F32)

    rows_out[...] = total.reshape(QA, 2, 8, D)
    low = lax.broadcasted_iota(jnp.int32, (8, D), 0) < 4
    for f in range(FR):
        for pair in range(3):
            lo = rows_out[(2 * pair + QA - core) % QA, f // 2]
            hi = rows_out[(2 * pair + 1 + QA - core) % QA, f // 2] if pair < 2 else lo
            if f % 2 == 0:
                rows_ = jnp.where(low, lo, pltpu.roll(hi, 4, 0))
            else:
                rows_ = jnp.where(low, pltpu.roll(lo, 4, 0), hi)
            out[f, pl.ds(8 * pair, 8), :] = rows_


def on_device(tokens, norm_gain, norm_shift, w_qkv, output_weight):
    vmem = pl.BlockSpec(memory_space=pltpu.VMEM)
    hbm = pl.BlockSpec(memory_space=pl.ANY)
    dma = pltpu.SemaphoreType.DMA
    rows = pl.pallas_call(
        kernel,
        out_shape=jax.ShapeDtypeStruct((FR, 24, D), F32),
        in_specs=[hbm, vmem, vmem, hbm, hbm],
        out_specs=vmem,
        scratch_shapes=[
            pltpu.VMEM((FR, PATCHES, D), BF16),
            pltpu.VMEM((3 * HD, D), BF16),
            pltpu.VMEM((HD, D), BF16),
            pltpu.VMEM((384, D), BF16),
            pltpu.VMEM((FR, HALF, 384), F32),
            pltpu.VMEM((BLOCKS, 2, TA, 16, 128), BF16),
            pltpu.VMEM((NT, TA, 16, 128), BF16),
            pltpu.VMEM((NT, RT, 16, 128), BF16),
            pltpu.VMEM((NH, RT, 16, 128), BF16),
            pltpu.VMEM((NH, 128, D), BF16),
            pltpu.VMEM((QA, 2, 8, D), F32),
            dma((2,)),
            dma((2,)),
            dma((2, 2 * BLOCKS)),
            dma((2,)),
            dma((3, NT)),
            dma((1,)),
            dma((18,)),
            dma((18,)),
        ],
        compiler_params=pltpu.CompilerParams(
            collective_id=0, has_side_effects=True, vmem_limit_bytes=60 * 1024 * 1024
        ),
        cost_estimate=pl.CostEstimate(
            flops=2 * FR * PATCHES * D * 264 + 2 * 72 * D * D,
            bytes_accessed=5_000_000,
            transcendentals=18 * 64 * 64,
        ),
    )(
        tokens,
        norm_gain,
        norm_shift,
        jnp.transpose(w_qkv, (1, 2, 0)).reshape(3 * HD, D),
        output_weight,
    )
    core = lax.axis_index("head") % 2
    return lax.dynamic_slice_in_dim(rows, 2 * core, 18, axis=1).astype(BF16)


def solution(mesh):
    return jax.shard_map(
        on_device,
        mesh=mesh,
        in_specs=(P("tm", None, None), P(), P(), P(None, "head", None), P("head", None)),
        out_specs=P("tm", "head", None),
        check_vma=False,
    )
```

time: 48.3 us -> 43.6 us (0.903)
  the two profiles are of different devices: /device:TPU:59 before, /device:TPU:1 now
where the time goes in v4:
time: 43.6 us; the launch traced here: 43.4 us
  Pallas kernels  41.6 us (95%)
  local copies, waits for them, and re-layouts  1.86 us (4%)
    pallas_call x1, Pallas kernels, on_device(): pl.pallas_call(kernel, out_shape=jax.ShapeDtypeStruct((FR, 24, D), F32),...  41.6 us
    convert_element_type x2, local copies, waits for them, and re-layouts, on_device(): return lax.dynamic_slice_in_dim(rows, 2 * core, 18, axis=1).astype(BF16)  1.86 us

profile of v4, /device:TPU:1, one launch (start us, length us, event | category | flops | bytes accessed | tf_op | source)
XLA Modules:
  0.0 43.4 jit_solution(9709769678245251709)
XLA Ops:
  0.0 41.6 %shard_map.55 = f32[4,24,1408]{2,1,0:T(8,128)} custom-call(bf16[4,288,1408]{2,1,0:T(8,128)(2,1)} %tok_hbm.1, f32[1408]{0:T(1024)} %gain_row.1, f32[1408]{0:T(1024)} %shift_row.1, bf16[264,1408]{1,0:T(8,128)(2,1)} %bitcast.3, bf16[88,1408]{1,0:T(8,128)(2,1)} %wo_hbm.1), custom_call_target="tpu_custom_call" | custom-call | flops 1141899264 | bytes 5000000 | tf_op jit(solution)/shard_map/pallas_call | solution.py:430
  41.6 1.1 %dynamic-slice_convert_fusion = bf16[4,18,1408]{2,1,0:T(8,128)(2,1)S(1)} fusion(f32[4,24,1408]{2,1,0:T(8,128)} %shard_map.55, s32[]{:T(128)S(6)} %select_n.11), kind=kLoop, calls=%fused_computation | loop fusion | bytes 405508 | tf_op jit(solution)/shard_map/convert_element_type | solution.py:472
  42.7 0.8 %copy.7 = bf16[4,18,1408]{2,0,1:T(4,128)(2,1)} copy(bf16[4,18,1408]{2,1,0:T(8,128)(2,1)S(1)} %dynamic-slice_convert_fusion) | data formatting | bytes 405504 | tf_op jit(solution)/shard_map/convert_element_type | solution.py:472

commit v5 on v4

--- a/solution.py
+++ b/solution.py
@@ -28,8 +28,8 @@
 
 
 def kernel(
-    tok_hbm, gain_row, shift_row, wq_hbm, wo_hbm, out,
-    tok, wq, wo, wperm, packed, send, recv, ret_send, ret_recv, wbuf, rows_out,
+    tok_hbm, gain_hbm, shift_hbm, wq_hbm, wo_hbm, out,
+    tok, gain_row, shift_row, wq, wo, wperm, packed, send, recv, ret_send, ret_recv, wbuf, rows_out,
     tok_sem, in_sem, p1_send, p1_recv, rt_send, rt_recv, w_send, w_recv,
 ):
     t = lax.axis_index("tm")
@@ -55,8 +55,12 @@
     ]
     wq_copy = pltpu.make_async_copy(wq_hbm, wq, in_sem.at[0])
     wo_copy = pltpu.make_async_copy(wo_hbm, wo, in_sem.at[1])
+    gain_copy = pltpu.make_async_copy(gain_hbm, gain_row, in_sem.at[2])
+    shift_copy = pltpu.make_async_copy(shift_hbm, shift_row, in_sem.at[3])
     tok_copies[0].start()
     wq_copy.start()
+    gain_copy.start()
+    shift_copy.start()
     tok_copies[1].start()
     wo_copy.start()
 
@@ -78,6 +82,8 @@
     wperm[...] = jnp.concatenate(
         [w[0:88], w[176:216], w[88:176], w[216:264], jnp.zeros((120, D), F32)], axis=0
     ).astype(BF16)
+    gain_copy.wait()
+    shift_copy.wait()
     gain = gain_row[...].reshape(1, D)
     shift = shift_row[...].reshape(1, D)
 
@@ -410,17 +416,15 @@
     )
     total = jnp.dot(left, wbuf[...].reshape(NH * 128, D), preferred_element_type=F32)
 
-    rows_out[...] = total.reshape(QA, 2, 8, D)
-    low = lax.broadcasted_iota(jnp.int32, (8, D), 0) < 4
-    for f in range(FR):
-        for pair in range(3):
-            lo = rows_out[(2 * pair + QA - core) % QA, f // 2]
-            hi = rows_out[(2 * pair + 1 + QA - core) % QA, f // 2] if pair < 2 else lo
-            if f % 2 == 0:
-                rows_ = jnp.where(low, lo, pltpu.roll(hi, 4, 0))
-            else:
-                rows_ = jnp.where(low, pltpu.roll(lo, 4, 0), hi)
-            out[f, pl.ds(8 * pair, 8), :] = rows_
+    for c in range(D // 128):
+        rows_out[c] = total[:, 128 * c : 128 * c + 128]
+    for o in range(18):
+        at = o + 2 * core
+        quad = (at // 4 + QA - core) % QA
+        for c in range(D // 128):
+            out[o, :, pl.ds(128 * c, 128)] = rows_out[
+                c, pl.ds(16 * quad + at % 4, FR, stride=4), :
+            ].astype(BF16)
 
 
 def on_device(tokens, norm_gain, norm_shift, w_qkv, output_weight):
@@ -429,11 +433,13 @@
     dma = pltpu.SemaphoreType.DMA
     rows = pl.pallas_call(
         kernel,
-        out_shape=jax.ShapeDtypeStruct((FR, 24, D), F32),
-        in_specs=[hbm, vmem, vmem, hbm, hbm],
+        out_shape=jax.ShapeDtypeStruct((18, FR, D), BF16),
+        in_specs=[hbm] * 5,
         out_specs=vmem,
         scratch_shapes=[
             pltpu.VMEM((FR, PATCHES, D), BF16),
+            pltpu.VMEM((D,), F32),
+            pltpu.VMEM((D,), F32),
             pltpu.VMEM((3 * HD, D), BF16),
             pltpu.VMEM((HD, D), BF16),
             pltpu.VMEM((384, D), BF16),
@@ -443,9 +449,9 @@
             pltpu.VMEM((NT, RT, 16, 128), BF16),
             pltpu.VMEM((NH, RT, 16, 128), BF16),
             pltpu.VMEM((NH, 128, D), BF16),
-            pltpu.VMEM((QA, 2, 8, D), F32),
+            pltpu.VMEM((D // 128, 16 * QA, 128), F32),
             dma((2,)),
-            dma((2,)),
+            dma((4,)),
             dma((2, 2 * BLOCKS)),
             dma((2,)),
             dma((3, NT)),
@@ -454,7 +460,7 @@
             dma((18,)),
         ],
         compiler_params=pltpu.CompilerParams(
-            collective_id=0, has_side_effects=True, vmem_limit_bytes=60 * 1024 * 1024
+            collective_id=0, has_side_effects=True, vmem_limit_bytes=55000 * 1024
         ),
         cost_estimate=pl.CostEstimate(
             flops=2 * FR * PATCHES * D * 264 + 2 * 72 * D * D,
@@ -468,8 +474,7 @@
         jnp.transpose(w_qkv, (1, 2, 0)).reshape(3 * HD, D),
         output_weight,
     )
-    core = lax.axis_index("head") % 2
-    return lax.dynamic_slice_in_dim(rows, 2 * core, 18, axis=1).astype(BF16)
+    return jnp.transpose(rows, (1, 0, 2))
 
 
 def solution(mesh):

time: 43.6 us -> 42.1 us (0.966)
  Pallas kernels: 41.6 us -> 39.8 us
    unnamed x0 -> x5, local copies, waits for them, and re-layouts: none -> 2.07 us
    convert_element_type x2 -> x0, local copies, waits for them, and re-layouts: 1.86 us -> none  [on_device(): return lax.dynamic_slice_in_dim(rows, 2 * core, 18, axis=1).astype(BF16)]
    pallas_call x1, Pallas kernels: 41.6 us -> 39.8 us  [on_device(): pl.pallas_call(kernel, out_shape=jax.ShapeDtypeStruct((18, FR, D), BF16),...]
where the time goes in v5:
time: 42.1 us; the launch traced here: 41.9 us
  Pallas kernels  39.8 us (95%)
  local copies, waits for them, and re-layouts  2.07 us (5%)
    pallas_call x1, Pallas kernels, on_device(): pl.pallas_call(kernel, out_shape=jax.ShapeDtypeStruct((18, FR, D), BF16),...  39.8 us
    unnamed x5, local copies, waits for them, and re-layouts  2.07 us

profile of v5, /device:TPU:1, one launch (start us, length us, event | category | flops | bytes accessed | tf_op | source)
XLA Modules:
  0.0 41.9 jit_solution(6415062697841130746)
XLA Ops:
  0.0 0.0 copy-start
  0.0 0.7 %copy-done = f32[1408]{0:T(1024)S(1)} copy-done((f32[1408]{0:T(1024)S(1)}, f32[1408]{0:T(1024)}, u32[]{:S(2)}) %copy-start) | copy-done | bytes 5656
  0.7 0.0 copy-start.1
  0.7 0.7 %copy-done.1 = f32[1408]{0:T(1024)S(1)} copy-done((f32[1408]{0:T(1024)S(1)}, f32[1408]{0:T(1024)}, u32[]{:S(2)}) %copy-start.1) | copy-done | bytes 5656
  1.4 39.8 %shard_map.55 = bf16[18,4,1408]{2,1,0:T(4,128)(2,1)S(1)} custom-call(bf16[4,288,1408]{2,1,0:T(8,128)(2,1)} %tok_hbm.1, f32[1408]{0:T(1024)S(1)} %copy-done, f32[1408]{0:T(1024)S(1)} %copy-done.1, bf16[264,1408]{1,0:T(8,128)(2,1)} %bitcast.5, bf16[88,1408]{1,0:T(8,128)(2,1)} %wo_hbm.1), custom_call_target="tpu_custom_call" | custom-call | flops 1141899264 | bytes 5000000 | tf_op jit(solution)/shard_map/pallas_call | solution.py:434
  41.2 0.7 %copy.7 = bf16[4,18,1408]{2,0,1:T(4,128)(2,1)} copy(bf16[4,18,1408]{2,0,1:T(4,128)(2,1)S(1)} %bitcast.4) | data formatting | bytes 405504
Async XLA Ops:
  0.0 0.7 %copy-start = (f32[1408]{0:T(1024)S(1)}, f32[1408]{0:T(1024)}, u32[]{:S(2)}) copy-start(f32[1408]{0:T(1024)} %gain_hbm.1) | copy-start | bytes 16900
  0.7 0.7 %copy-start.1 = (f32[1408]{0:T(1024)S(1)}, f32[1408]{0:T(1024)}, u32[]{:S(2)}) copy-start(f32[1408]{0:T(1024)} %shift_hbm.1) | copy-start | bytes 16900

commit v6 on v5

--- a/solution.py
+++ b/solution.py
@@ -89,18 +89,15 @@
 
     def project(n):
         tok_copies[n].wait()
-
-        @pl.loop(0, FR)
-        def _(f):
-            values = tok[f, half_rows(n), :].astype(F32)
-            average = jnp.mean(values, axis=-1, keepdims=True)
-            centred = values - average
-            var = jnp.mean(centred * centred, axis=-1, keepdims=True)
-            normed = centred * lax.rsqrt(var + 1e-06) * gain + shift
-            tok[f, half_rows(n), :] = normed.astype(BF16)
+        values = tok[:, half_rows(n), :].reshape(FR * HALF, D).astype(F32)
+        average = jnp.mean(values, axis=-1, keepdims=True)
+        centred = values - average
+        var = jnp.mean(centred * centred, axis=-1, keepdims=True)
+        normed = centred * lax.rsqrt(var + 1e-06) * gain + shift
+        normed = normed.astype(BF16)
 
         packed[...] = lax.dot_general(
-            tok[:, half_rows(n), :].reshape(FR * HALF, D), wperm[...],
+            normed, wperm[...],
             (((1,), (1,)), ((), ())), preferred_element_type=F32,
         ).reshape(FR, HALF, 384)
 
@@ -469,8 +466,8 @@
         ),
     )(
         tokens,
-        norm_gain,
-        norm_shift,
+        pltpu.with_memory_space_constraint(norm_gain, pltpu.HBM),
+        pltpu.with_memory_space_constraint(norm_shift, pltpu.HBM),
         jnp.transpose(w_qkv, (1, 2, 0)).reshape(3 * HD, D),
         output_weight,
     )

time: 42.1 us -> 40.4 us (0.960)
  local copies, waits for them, and re-layouts: 2.07 us -> 0.68 us
    unnamed x5 -> x1, local copies, waits for them, and re-layouts: 2.07 us -> 0.68 us
where the time goes in v6:
time: 40.4 us; the launch traced here: 40.3 us
  Pallas kernels  39.6 us (98%)
  local copies, waits for them, and re-layouts  0.68 us (2%)
    pallas_call x1, Pallas kernels, on_device(): pl.pallas_call(kernel, out_shape=jax.ShapeDtypeStruct((18, FR, D), BF16),...  39.6 us

profile of v6, /device:TPU:1, one launch (start us, length us, event | category | flops | bytes accessed | tf_op | source)
XLA Modules:
  0.0 40.3 jit_solution(14640186238632273859)
XLA Ops:
  0.0 39.6 %shard_map.55 = bf16[18,4,1408]{2,1,0:T(4,128)(2,1)S(1)} custom-call(bf16[4,288,1408]{2,1,0:T(8,128)(2,1)} %tok_hbm.1, f32[1408]{0:T(1024)} %gain_hbm.1, f32[1408]{0:T(1024)} %shift_hbm.1, bf16[264,1408]{1,0:T(8,128)(2,1)} %bitcast.5, bf16[88,1408]{1,0:T(8,128)(2,1)} %wo_hbm.1), custom_call_target="tpu_custom_call" | custom-call | flops 1141899264 | bytes 5000000 | tf_op jit(solution)/shard_map/pallas_call | solution.py:431
  39.7 0.7 %copy.7 = bf16[4,18,1408]{2,0,1:T(4,128)(2,1)} copy(bf16[4,18,1408]{2,0,1:T(4,128)(2,1)S(1)} %bitcast.4) | data formatting | bytes 405504

commit v7 on v6

--- a/solution.py
+++ b/solution.py
@@ -39,6 +39,19 @@
     y, xl = chip // 2, chip % 2
     is_a = xh == core
 
+    def head_of(y_, xl_, core_):
+        return ((y_ + 4) % 4) * 4 + xl_ * 2 + core_
+
+    x_cross = ((1 - xh) * NZ + z, head_of(y, 1 - xl, core))
+    barrier = pltpu.get_barrier_semaphore()
+
+    @pl.loop(1, NT)
+    def _(k):
+        pl.semaphore_signal(barrier, inc=1, device_id=((t + k) % NT, h), device_id_type=MESH)
+        pl.semaphore_signal(barrier, inc=1, device_id=(t, (h + k) % NH), device_id_type=MESH)
+
+    pl.semaphore_signal(barrier, inc=1, device_id=x_cross, device_id_type=MESH)
+
     halves = ((z + xl) % 2, (z + xl + 1) % 2)
 
     def z_of(block, y_, xl_):
@@ -59,23 +72,10 @@
     shift_copy = pltpu.make_async_copy(shift_hbm, shift_row, in_sem.at[3])
     tok_copies[0].start()
     wq_copy.start()
+    wo_copy.start()
     gain_copy.start()
     shift_copy.start()
     tok_copies[1].start()
-    wo_copy.start()
-
-    def head_of(y_, xl_, core_):
-        return ((y_ + 4) % 4) * 4 + xl_ * 2 + core_
-
-    x_cross = ((1 - xh) * NZ + z, head_of(y, 1 - xl, core))
-    barrier = pltpu.get_barrier_semaphore()
-
-    @pl.loop(1, NT)
-    def _(k):
-        pl.semaphore_signal(barrier, inc=1, device_id=((t + k) % NT, h), device_id_type=MESH)
-        pl.semaphore_signal(barrier, inc=1, device_id=(t, (h + k) % NH), device_id_type=MESH)
-
-    pl.semaphore_signal(barrier, inc=1, device_id=x_cross, device_id_type=MESH)
 
     wq_copy.wait()
     w = wq[...].astype(F32)
@@ -242,9 +242,6 @@
         ):
             w_wait(slot(dy, other_x, 1), FULL, n)
 
-    project(0)
-    pl.semaphore_wait(barrier, 2 * (NT - 1) + 1)
-    start_first(0)
     wo_copy.wait()
     wbuf[h, pl.ds(0, WROWS), :] = jnp.concatenate(
         [wo[...].astype(F32), jnp.zeros((WROWS - HD, D), F32)], axis=0
@@ -254,7 +251,10 @@
     def _(k):
         wbuf[k, pl.ds(WROWS, 128 - WROWS), :] = jnp.zeros((128 - WROWS, D), BF16)
 
+    project(0)
+    pl.semaphore_wait(barrier, 2 * (NT - 1) + 1)
     w_first()
+    start_first(0)
     project(1)
     start_first(1)
     start_second(0)

time: 40.4 us -> 40.4 us (level)
  no operation moved by 1% of the time
where the time goes in v7:
time: 40.4 us; the launch traced here: 40.3 us
  Pallas kernels  39.6 us (98%)
  local copies, waits for them, and re-layouts  0.68 us (2%)
    pallas_call x1, Pallas kernels, on_device(): pl.pallas_call(kernel, out_shape=jax.ShapeDtypeStruct((18, FR, D), BF16),...  39.6 us

profile of v7, /device:TPU:1, one launch (start us, length us, event | category | flops | bytes accessed | tf_op | source)
XLA Modules:
  0.0 40.3 jit_solution(10380197199102203027)
XLA Ops:
  0.0 39.6 %shard_map.55 = bf16[18,4,1408]{2,1,0:T(4,128)(2,1)S(1)} custom-call(bf16[4,288,1408]{2,1,0:T(8,128)(2,1)} %tok_hbm.1, f32[1408]{0:T(1024)} %gain_hbm.1, f32[1408]{0:T(1024)} %shift_hbm.1, bf16[264,1408]{1,0:T(8,128)(2,1)} %bitcast.5, bf16[88,1408]{1,0:T(8,128)(2,1)} %wo_hbm.1), custom_call_target="tpu_custom_call" | custom-call | flops 1141899264 | bytes 5000000 | tf_op jit(solution)/shard_map/pallas_call | solution.py:431
  39.6 0.7 %copy.7 = bf16[4,18,1408]{2,0,1:T(4,128)(2,1)} copy(bf16[4,18,1408]{2,0,1:T(4,128)(2,1)S(1)} %bitcast.4) | data formatting | bytes 405504

commit v8 on v7

--- a/solution.py
+++ b/solution.py
@@ -348,16 +348,10 @@
     @pl.when(is_a)
     def _():
         p1_wait(1, SECOND[0])
-        put(3, straight(attend(4), 4))
-
-    @pl.when(jnp.logical_not(is_a))
-    def _():
-        p1_wait(1, SECOND[1])
-
-    put(2, jnp.where(lane < HD, straight(attend(3), 3), rest2))
-
-    @pl.when(is_a)
-    def _():
+        mixed3, mixed4 = attend(3), attend(4)
+        put(2, jnp.where(lane < HD, straight(mixed3, 3), rest2))
+        put(3, straight(mixed4, 4))
+
         @pl.loop(0, NT)
         def _(k):
             to_t = far_first(k)
@@ -366,6 +360,9 @@
 
     @pl.when(jnp.logical_not(is_a))
     def _():
+        p1_wait(1, SECOND[1])
+        put(2, jnp.where(lane < HD, straight(attend(3), 3), rest2))
+
         @pl.loop(0, NT)
         def _(k):
             start(ret_second_b(far_first(k)))

time: 40.4 us -> 40.7 us (level)
  no operation moved by 1% of the time
where the time goes in v8:
time: 40.7 us; the launch traced here: 40.6 us
  Pallas kernels  39.9 us (98%)
  local copies, waits for them, and re-layouts  0.68 us (2%)
    pallas_call x1, Pallas kernels, on_device(): pl.pallas_call(kernel, out_shape=jax.ShapeDtypeStruct((18, FR, D), BF16),...  39.9 us

profile of v8, /device:TPU:1, one launch (start us, length us, event | category | flops | bytes accessed | tf_op | source)
XLA Modules:
  0.0 40.6 jit_solution(11976720246048775146)
XLA Ops:
  0.0 39.9 %shard_map.55 = bf16[18,4,1408]{2,1,0:T(4,128)(2,1)S(1)} custom-call(bf16[4,288,1408]{2,1,0:T(8,128)(2,1)} %tok_hbm.1, f32[1408]{0:T(1024)} %gain_hbm.1, f32[1408]{0:T(1024)} %shift_hbm.1, bf16[264,1408]{1,0:T(8,128)(2,1)} %bitcast.5, bf16[88,1408]{1,0:T(8,128)(2,1)} %wo_hbm.1), custom_call_target="tpu_custom_call" | custom-call | flops 1141899264 | bytes 5000000 | tf_op jit(solution)/shard_map/pallas_call | solution.py:428
  39.9 0.7 %copy.7 = bf16[4,18,1408]{2,0,1:T(4,128)(2,1)} copy(bf16[4,18,1408]{2,0,1:T(4,128)(2,1)S(1)} %bitcast.4) | data formatting | bytes 405504
